TPU v7x, 32 devices: a whole 2x2x4 slice. The times are simulated.
32 devices in a mesh: energy: 8 (over y, x, core), cell: 4 (over z).
Axes of the slice: x: 2, y: 2, z: 4, core: 2. Of those that a mesh axis runs over, the one named last changes fastest.
Arguments:
- retarded_diag: bfloat16 [2, 16, 16, 256, 256], P(None, 'energy', 'cell'), may hold values from -0.375 to 0.375
- retarded_lower: bfloat16 [2, 16, 16, 256, 256], P(None, 'energy', 'cell'), may hold values from -0.375 to 0.375
- retarded_upper: bfloat16 [2, 16, 16, 256, 256], P(None, 'energy', 'cell'), may hold values from -0.375 to 0.375
- sigma_lesser: bfloat16 [2, 16, 16, 256, 256], P(None, 'energy', 'cell'), may hold values from -6 to 6
- screened: bfloat16 [2, 16, 32], P(None, 'cell'), may hold values from -1 to 1
- kept: int32 [16, 8], P('cell'), may hold values from 0 to 15, as said below
- kept_count: int32 [16], P('cell'), may hold values from 1 to 8, as said below
Outputs:
- sigma_new: bfloat16 [2, 16, 16, 8, 4096], P(None, 'energy', 'cell')
Inputs may be any that keep to these rules, and one draw needn't show every extreme that they name: `kept`: each row holds 8 different sub-block numbers. `kept_count`: some cell has 8 live slots and some other cell 1.
All inputs are finite; a program needn't handle non-finite values.
Results may differ from a plain program's by a relative error of at most 0.0057.
Values may be sent and summed in bfloat16 or wider, within the bound.
No kernel may reach another device: no remote copies, remote signals or barrier semaphores. Data moves between devices by JAX's collectives and lax.ppermute only.
A program may use at most 128 MiB of HBM per device.

v0:
```python
from functools import partial

import jax
import jax.numpy as jnp
from jax import lax
from jax.experimental import pallas as pl
from jax.experimental.pallas import tpu as pltpu
from jax.sharding import PartitionSpec as P

SUB = 64
LANES = 2 * SUB
PAIRS = SUB // 2
STEP = 8


def pairwise(devices):
    return devices <= STEP and devices & (devices - 1) == 0


def partners(devices):
    if not pairwise(devices):
        return list(range(devices))
    others = sorted(
        range(1, devices), key=lambda bits: (-bin(bits >> 1).count("1"), bits & 1, bits)
    )
    return [0] + others


def partner_of(bits, devices):
    if not pairwise(devices):
        return bits
    return lax.axis_index("energy") ^ bits


def exchange(parts):
    devices = len(parts)
    if not pairwise(devices):
        sent = lax.all_to_all(jnp.stack(parts), "energy", split_axis=0, concat_axis=0, tiled=True)
        return [sent[index] for index in range(devices)]
    return [parts[0]] + [
        lax.ppermute(part, "energy", [(source, source ^ bits) for source in range(devices)])
        for bits, part in zip(partners(devices)[1:], parts[1:])
    ]


def packing_order(cell_count):
    interior = list(range(1, cell_count - 1))
    return interior + [0, cell_count - 1] if cell_count > 1 else [0]


def slot_base(count_ref, order, position):
    base = jnp.int32(0)
    for place, cell in enumerate(order[:-1]):
        base = base + jnp.where(place < position, count_ref[cell], 0)
    return base


def inner_products(factor, middle_r, middle_i):
    row = jnp.concatenate([factor[0], factor[1]], axis=1)
    real_part = jnp.dot(
        row, jnp.concatenate([middle_r, -middle_i], axis=0), preferred_element_type=jnp.float32
    )
    imag_part = jnp.dot(
        row, jnp.concatenate([middle_i, middle_r], axis=0), preferred_element_type=jnp.float32
    )
    return by_strips(real_part.astype(jnp.bfloat16), imag_part.astype(jnp.bfloat16))


def by_strips(real_part, imag_part):
    pieces = []
    for start in range(0, real_part.shape[0], SUB):
        pieces += [real_part[start : start + SUB], imag_part[start : start + SUB]]
    return jnp.concatenate(pieces, axis=0)


def paired_rows(product_ref, number, group):
    def rows(half, odd):
        start = half * SUB + group * 2 * STEP + odd
        return product_ref[number, pl.ds(start, STEP, stride=2), :]

    left = lax.broadcasted_iota(jnp.int32, (STEP, LANES), 1) < SUB
    top_even, top_odd = rows(0, 0), rows(0, 1)
    low_even, low_odd = rows(1, 0), rows(1, 1)
    real_part = jnp.where(left, top_even, low_odd) + pltpu.roll(
        jnp.where(left, top_odd, low_even), SUB, 1
    )
    imag_part = jnp.where(left, low_even, -top_odd) + pltpu.roll(
        jnp.where(left, low_odd, -top_even), SUB, 1
    )
    return real_part, imag_part


def sandwiches(factors, middles):
    inner = jnp.concatenate(
        [inner_products(factor, *middle) for factor, middle in zip(factors, middles)], axis=1
    )
    return lax.dot_general(
        inner,
        jnp.concatenate([by_strips(*factor) for factor in factors], axis=1),
        (((1,), (1,)), ((), ())),
        preferred_element_type=jnp.float32,
    )


def stage_slots(products, kept_ref, cell, energy, devices, tile_rows, product, staged):
    per_side = products.shape[0] // LANES
    share = PAIRS // devices
    for top in range(per_side):
        for side in range(per_side):
            product[top * per_side + side] = products[
                top * LANES : (top + 1) * LANES, side * LANES : (side + 1) * LANES
            ]
    for slot in range(kept_ref.shape[1]):
        number = kept_ref[cell, slot]
        for group in range(PAIRS // STEP):
            pair = paired_rows(product, number, group)
            device = (group * STEP) % devices
            for part in range(2):
                row = (energy * 2 + part) * share + group * STEP // devices
                start = device * tile_rows + row
                staged[slot, pl.ds(start, STEP, stride=tile_rows), :] = pair[part]


def slot_tiles(staged, slot, out_ref):
    devices, _, tile_rows, _ = out_ref.shape
    return staged[slot].reshape(devices, tile_rows, LANES).astype(jnp.bfloat16)


def local_kernel(order, devices, sizes, kept_ref, count_ref, screened_ref, *refs):
    sources, sigma_source = refs[:3], refs[3]
    out_ref, partial_ref, outer_ref, weight_ref, index_ref = refs[4:9]
    held, near, sigma, table, product, staged, held_sem, near_sem, outer_sem, sigma_sem = refs[9:]
    _, energies, cell_count, _, _ = sigma_source.shape
    slots = kept_ref.shape[1]
    last = cell_count - 1
    steps = (cell_count - 2) * energies
    diag, lower, upper = sources

    def held_copies(step):
        position, energy = step // energies, step % energies
        return [
            pltpu.make_async_copy(
                source.at[:, energy, position + 1],
                held.at[term, :, energy, position],
                held_sem.at[term, step],
            )
            for term, source in enumerate(sources)
        ]

    def sigma_copy(energy):
        return pltpu.make_async_copy(
            sigma_source.at[:, energy], sigma.at[:, energy], sigma_sem.at[energy]
        )

    def near_copies(edge, energy):
        return [
            pltpu.make_async_copy(
                source.at[:, energy, edge * last],
                near.at[term, :, energy, edge],
                near_sem.at[term, energy, edge],
            )
            for term, source in enumerate((diag, (upper, lower)[edge]))
        ]

    def outer_copy(edge, energy):
        return pltpu.make_async_copy(
            (lower, upper)[edge].at[:, energy, edge * last],
            outer_ref.at[:, energy, edge],
            outer_sem.at[energy, edge],
        )

    ahead = min(energies, steps)
    for step in range(ahead):
        sigma_copy(step % energies).start()
        for copy in held_copies(step):
            copy.start()
    live = jnp.int32(0)
    for cell in range(cell_count):
        live = live + count_ref[cell]
    index = jnp.int32(0)
    for size in sizes[:-1]:
        index = index + jnp.where(live > size, 1, 0)
    index_ref[0] = index
    fill_mixing(screened_ref, weight_ref, table)

    def pair_of(ref, energy, spot):
        return ref[0, energy, spot], ref[1, energy, spot]

    def inside(step, _):
        position, energy = step // energies, step % energies
        cell = position + 1

        @pl.when(step + ahead < steps)
        def _():
            for copy in held_copies(step + ahead):
                copy.start()

        @pl.when(step == ahead - 1)
        def _():
            for edge in range(2):
                for other in range(energies):
                    for copy in near_copies(edge, other):
                        copy.start()
                    outer_copy(edge, other).start()

        @pl.when(position == 0)
        def _():
            sigma_copy(energy).wait()

        for copy in held_copies(step):
            copy.wait()
        products = sandwiches(
            [pair_of(held.at[term], energy, position) for term in range(3)],
            [pair_of(sigma, energy, other) for other in (cell, cell - 1, cell + 1)],
        )
        stage_slots(products, kept_ref, cell, energy, devices, out_ref.shape[2], product, staged)

        @pl.when(energy == energies - 1)
        def _():
            base = slot_base(count_ref, order, position)
            for slot in range(slots):
                out_ref[:, base + slot] = slot_tiles(staged, slot, out_ref)

        return 0

    lax.fori_loop(0, steps, inside, 0)
    for edge, cells in enumerate(((0, 1), (last, last - 1))):

        def beside(energy, _, edge=edge, cells=cells):
            for copy in near_copies(edge, energy):
                copy.wait()
            partial_ref[edge, energy] = sandwiches(
                [pair_of(near.at[term], energy, edge) for term in range(2)],
                [pair_of(sigma, energy, cell) for cell in cells],
            )
            return 0

        lax.fori_loop(0, energies, beside, 0)
    for edge in range(2):
        for energy in range(energies):
            outer_copy(edge, energy).wait()


def edge_kernel(
    order, kept_ref, count_ref, partial_ref, outer_ref, halo_first, halo_second, earlier, *refs
):
    *outs, out_ref, product, staged = refs
    _, energies, edge_count, _, _ = outer_ref.shape
    devices, total, tile_rows, _ = out_ref.shape
    ready = min(earlier.shape[1], total)
    out_ref[:, :ready] = earlier[:, :ready]
    odd = lax.axis_index("cell") % 2
    for edge, halo in ((1 - odd, halo_first), (odd, halo_second)):
        position = len(order) - edge_count + edge
        cell = edge * (len(order) - 1)
        base = slot_base(count_ref, order, position)
        for energy in range(energies):
            products = partial_ref[edge, energy] + sandwiches(
                [(outer_ref[0, energy, edge], outer_ref[1, energy, edge])],
                [(halo[0, energy, 0], halo[1, energy, 0])],
            )
            stage_slots(
                products, kept_ref, cell, energy, devices, tile_rows, product.at[energy], staged
            )
        for slot in range(kept_ref.shape[1]):

            @pl.when(slot < count_ref[cell])
            def _(slot=slot, base=base):
                out_ref[:, base + slot] = slot_tiles(staged, slot, out_ref)

    for bits, out in zip(partners(devices), outs):
        out[...] = out_ref[partner_of(bits, devices)]


SCALARS = pl.BlockSpec(memory_space=pltpu.SMEM)
VECTORS = pl.BlockSpec(memory_space=pltpu.VMEM)
STAYING = pl.BlockSpec(memory_space=pltpu.HBM)


def cost_of(places, energies, size):
    return pl.CostEstimate(
        flops=places * energies * 48 * size**3,
        bytes_accessed=places * energies * 6 * size * size * 4,
        transcendentals=0,
    )


def fill_scratch(size, slots, rows):
    return [
        pltpu.VMEM(((size // SUB) ** 2, LANES, LANES), jnp.float32),
        pltpu.VMEM((slots, rows, LANES), jnp.float32),
    ]


def local_part(blocks, screened, kept, kept_count, devices, sizes):
    _, energies, cells, size, _ = blocks[0].shape
    slots = kept.shape[1]
    share = PAIRS // devices
    tile_rows = energies * 2 * share
    rows = 2 * screened.shape[2] // 2 * share
    places = cells - 2
    wide = 2 * size

    def bfloat(*shape):
        return jax.ShapeDtypeStruct(shape, jnp.bfloat16)

    return pl.pallas_call(
        partial(local_kernel, packing_order(cells), devices, sizes),
        in_specs=[SCALARS, SCALARS, VECTORS] + [STAYING] * 4,
        out_specs=[VECTORS] * 4 + [SCALARS],
        out_shape=[
            bfloat(devices, places * slots, tile_rows, LANES),
            jax.ShapeDtypeStruct((2, energies, wide, wide), jnp.float32),
            bfloat(2, energies, 2, size, size),
            bfloat(cells, rows, rows),
            jax.ShapeDtypeStruct((1,), jnp.int32),
        ],
        scratch_shapes=[
            pltpu.VMEM((3, 2, energies, places, size, size), jnp.bfloat16),
            pltpu.VMEM((2, 2, energies, 2, size, size), jnp.bfloat16),
            pltpu.VMEM((2, energies, cells, size, size), jnp.bfloat16),
            pltpu.VMEM((cells, 2 * share, 2 * rows), jnp.float32),
        ]
        + fill_scratch(size, slots, devices * tile_rows)
        + [
            pltpu.SemaphoreType.DMA((3, energies * places)),
            pltpu.SemaphoreType.DMA((2, energies, 2)),
            pltpu.SemaphoreType.DMA((energies, 2)),
            pltpu.SemaphoreType.DMA((energies,)),
        ],
        compiler_params=pltpu.CompilerParams(vmem_limit_bytes=55 << 20),
        cost_estimate=cost_of(cells, energies, size),
    )(kept, kept_count, screened, *blocks)


def edges(total, partial_sum, outer, halo, earlier, kept, kept_count):
    _, energies, _, size, _ = outer.shape
    devices, _, tile_rows, _ = earlier.shape
    return pl.pallas_call(
        partial(edge_kernel, packing_order(kept.shape[0])),
        in_specs=[SCALARS, SCALARS] + [VECTORS] * 5,
        out_specs=[VECTORS] * devices,
        out_shape=[jax.ShapeDtypeStruct((total, tile_rows, LANES), jnp.bfloat16)] * devices,
        scratch_shapes=[pltpu.VMEM((devices, total, tile_rows, LANES), jnp.bfloat16)]
        + [
            pltpu.VMEM((energies, (size // SUB) ** 2, LANES, LANES), jnp.float32),
            pltpu.VMEM((kept.shape[1], devices * tile_rows, LANES), jnp.float32),
        ],
        compiler_params=pltpu.CompilerParams(vmem_limit_bytes=32 << 20),
        cost_estimate=cost_of(1, energies, size),
    )(kept, kept_count, partial_sum, outer, *halo, earlier)


def border_kernel(sigma, out, sem):
    cell = jnp.where(lax.axis_index("cell") % 2 == 1, 0, sigma.shape[2] - 1)
    copy = pltpu.make_async_copy(sigma.at[:, :, pl.ds(cell, 1)], out, sem)
    copy.start()
    copy.wait()


def border(sigma):
    return pl.pallas_call(
        border_kernel,
        in_specs=[STAYING],
        out_specs=VECTORS,
        out_shape=jax.ShapeDtypeStruct(sigma.shape[:2] + (1,) + sigma.shape[3:], sigma.dtype),
        scratch_shapes=[pltpu.SemaphoreType.DMA],
        compiler_params=pltpu.CompilerParams(vmem_limit_bytes=60 << 20),
    )(sigma)


def fill_mixing(screened_ref, weight_ref, table):
    _, cells, doubled = screened_ref.shape
    _, rows, lane_count = table.shape
    total, share = doubled // 2, rows // 2
    shape = (2 * doubled, lane_count)
    source = lax.broadcasted_iota(jnp.int32, shape, 0)
    lane = lax.broadcasted_iota(jnp.int32, shape, 1)
    offset = 2 * total - 2 - lane // rows
    part = (lane // share) % 2
    spot = lane % share
    both = jnp.concatenate([screened_ref[0], screened_ref[1]], axis=1)
    for row in range(rows):
        own_part, own_spot = row // share, row % share
        wanted = jnp.where(part == own_part, 0, doubled) + offset
        sign = jnp.where(part > own_part, -1.0, 1.0)
        pick = jnp.where((source == wanted) & (spot == own_spot) & (offset >= 0), sign, 0.0)
        table[:, row, :] = jnp.dot(
            both, pick.astype(jnp.bfloat16), preferred_element_type=jnp.float32
        )
    size = weight_ref.shape[1]
    for cell in range(cells):
        for energy in range(total):
            start = (total - 1 - energy) * rows
            weight_ref[cell, energy * rows : (energy + 1) * rows, :] = table[
                cell, :, start : start + size
            ].astype(jnp.bfloat16)


def mix_kernel(order, count_ref, weight_ref, *refs):
    parts, outs, x_ref, y_ref = refs[: len(refs) // 2 - 1], refs[len(refs) // 2 - 1 : -2], *refs[-2:]
    devices, total, tile_rows, _ = x_ref.shape
    for bits, part in zip(partners(devices), parts):
        x_ref[partner_of(bits, devices)] = part[...]
    ends = []
    end = jnp.int32(0)
    for cell in order[:-1]:
        end = end + count_ref[cell]
        ends.append(end)
    for slot in range(total):
        cell = jnp.int32(order[-1])
        for name, end in reversed(list(zip(order, ends))):
            cell = jnp.where(slot < end, name, cell)
        entries = x_ref[:, slot].reshape(devices * tile_rows, LANES)
        mixed = jnp.dot(weight_ref[cell], entries, preferred_element_type=jnp.float32)
        y_ref[:, slot] = mixed.astype(jnp.bfloat16).reshape(devices, tile_rows, LANES)
    for bits, out in zip(partners(devices), outs):
        out[...] = y_ref[partner_of(bits, devices)]


def mix(parts, weights, kept_count):
    devices = len(parts)
    return pl.pallas_call(
        partial(mix_kernel, packing_order(kept_count.shape[0])),
        in_specs=[SCALARS, VECTORS] + [VECTORS] * devices,
        out_specs=[VECTORS] * devices,
        out_shape=[jax.ShapeDtypeStruct(parts[0].shape, jnp.bfloat16)] * devices,
        scratch_shapes=[pltpu.VMEM((devices, *parts[0].shape), jnp.bfloat16)] * 2,
        compiler_params=pltpu.CompilerParams(vmem_limit_bytes=16 << 20),
    )(kept_count, weights, *parts)


def unpack_kernel(order, count_ref, *refs):
    *parts, out_ref, rows, cells_out, sems = refs
    devices = len(parts)
    total, tile_rows, _ = parts[0].shape
    pitch = tile_rows + 1
    _, energies, cell_count, slots, _ = out_ref.shape
    share = PAIRS // devices
    copies = []
    for position, cell in enumerate(order):
        base = slot_base(count_ref, order, position)
        held = rows.at[position % 2]
        for slot in range(slots):
            number = jnp.minimum(base + slot, total - 1)
            start = slot * pitch
            for bits, part in zip(partners(devices), parts):
                held[partner_of(bits, devices), start : start + tile_rows, :] = part[
                    number
                ].astype(jnp.float32)
        live = lax.broadcasted_iota(jnp.int32, (slots, LANES), 0) < count_ref[cell]
        for part in range(2):
            for energy in range(energies):
                for index in range(PAIRS):
                    row = (energy * 2 + part) * share + index // devices
                    entries = held[index % devices, pl.ds(row, slots, stride=pitch), :]
                    cells_out[part, energy, cell, :, index * LANES : (index + 1) * LANES] = (
                        jnp.where(live, entries, 0.0).astype(jnp.bfloat16)
                    )
        copy = pltpu.make_async_copy(cells_out.at[:, :, cell], out_ref.at[:, :, cell], sems.at[cell])
        copy.start()
        copies.append(copy)
    for copy in copies:
        copy.wait()


def unpack(parts, kept_count, energies, slots):
    devices = len(parts)
    cells = kept_count.shape[0]
    shape = (2, energies, cells, slots, SUB * SUB)
    return pl.pallas_call(
        partial(unpack_kernel, packing_order(cells)),
        in_specs=[SCALARS] + [VECTORS] * devices,
        out_specs=STAYING,
        out_shape=pltpu.HBM(shape, jnp.bfloat16),
        scratch_shapes=[
            pltpu.VMEM((2, devices, slots * (parts[0].shape[1] + 1), LANES), jnp.float32),
            pltpu.VMEM(shape, jnp.bfloat16),
            pltpu.SemaphoreType.DMA((cells,)),
        ],
        compiler_params=pltpu.CompilerParams(vmem_limit_bytes=16 << 20),
    )(kept_count, *parts)


def per_device(diag, lower, upper, sigma, screened, kept, kept_count):
    count = lax.axis_size("cell")
    devices = lax.axis_size("energy")
    outward = lax.axis_index("cell") % 2 * (sigma.shape[2] - 1)
    edge_cell = lax.dynamic_slice_in_dim(sigma, outward, 1, axis=2)

    def swap(block, start):
        pairs = [(low, low + 1) for low in range(start, count - 1, 2)]
        return lax.ppermute(block, "cell", pairs + [(high, low) for low, high in pairs])

    halo = swap(border(sigma), 0), swap(edge_cell, 1)
    energies, slots = sigma.shape[1], kept.shape[1]
    full = kept.shape[0] * slots
    sizes = [full * eighths // 8 for eighths in (4, 5, 6, 7, 8)]
    earlier, partial_sum, outer, weights, index = local_part(
        (diag, lower, upper, sigma), screened, kept, kept_count, devices, sizes
    )

    def with_slots(total, partial_sum, outer, halo, earlier, weights, kept, kept_count):
        parts = edges(total, partial_sum, outer, halo, earlier, kept, kept_count)
        mixed = mix(exchange(parts), weights, kept_count)
        return unpack(exchange(mixed), kept_count, energies, slots)

    return lax.switch(
        index[0],
        [partial(with_slots, size) for size in sizes],
        partial_sum, outer, halo, earlier, weights, kept, kept_count,
    )


def solution(mesh):
    placed = (
        P(None, "energy", "cell", None, None),
        P(None, "energy", "cell", None, None),
        P(None, "energy", "cell", None, None),
        P(None, "energy", "cell", None, None),
        P(None, "cell", None),
        P("cell", None),
        P("cell"),
    )
    return jax.shard_map(
        per_device,
        mesh=mesh,
        in_specs=placed,
        out_specs=P(None, "energy", "cell", None, None),
        check_vma=False,
    )
```

profile of v0, /device:TPU:17, one launch (start us, length us, event | category | flops | bytes accessed | tf_op | source)
XLA Modules:
  0.0 50.7 jit_solution(4004590538403477252)
XLA Ops:
  0.0 0.0 copy-start
  0.0 0.0 copy-start.1
  0.0 1.9 %shard_map.79 = bf16[2,2,1,256,256]{4,3,2,1,0:T(8,128)(2,1)} custom-call(bf16[2,2,4,256,256]{4,3,2,1,0:T(8,128)(2,1)} %sigma.1), custom_call_target="tpu_custom_call" | custom-call | tf_op jit(solution)/shard_map/pallas_call | solution.py:362
  1.9 1.4 %collective-permute-start.70 = (bf16[2,2,1,256,256]{4,3,2,1,0:T(8,128)(2,1)}, bf16[2,2,1,256,256]{4,3,2,1,0:T(8,128)(2,1)S(1)}, u32[]{:S(2)}, u32[]{:S(2)}) collective-permute-start(bf16[2,2,1,256,256]{4,3,2,1,0:T(8,128)(2,1)} %shard_map.79), channel_id=1, source_target_pairs={{0,1},{2,3},{1,0},{3,2},{4,5},{6,7},{5,4},{7,6},{8,9},{10,11},{9,8... | collective-permute-start | bytes 1572872 | tf_op jit(solution)/shard_map/ppermute | solution.py:493
  3.2 1.1 %constant_dynamic-slice_fusion = bf16[2,2,1,256,256]{4,3,2,1,0:T(8,128)(2,1)S(1)} fusion(bf16[2,2,4,256,256]{4,3,2,1,0:T(8,128)(2,1)} %sigma.1, s32[]{:T(128)S(6)} %select_n.11), kind=kLoop, calls=%fused_computation | loop fusion | bytes 1048580 | tf_op jit(solution)/shard_map/dynamic_slice | solution.py:489
  4.3 1.9 %collective-permute-start.71 = (bf16[2,2,1,256,256]{4,3,2,1,0:T(8,128)(2,1)S(1)}, bf16[2,2,1,256,256]{4,3,2,1,0:T(8,128)(2,1)S(1)}, u32[]{:S(2)}, u32[]{:S(2)}) collective-permute-start(bf16[2,2,1,256,256]{4,3,2,1,0:T(8,128)(2,1)S(1)} %constant_dynamic-slice_fusion), channel_id=1, source_target_pairs={{1,2},{2,1},{5,6},{6,5},{9,10},{10,9},{13,14},{14,13},{17,18},{18,... | collective-permute-start | bytes 1572872 | tf_op jit(solution)/shard_map/ppermute | solution.py:493
  6.3 0.0 copy-done
  6.3 0.0 copy-done.1
  6.3 10.7 %shard_map.78 = (bf16[8,16,16,128]{3,2,1,0:T(8,128)(2,1)S(1)}, f32[2,2,512,512]{3,2,1,0:T(8,128)S(1)}, bf16[2,2,2,256,256]{4,3,2,1,0:T(8,128)(2,1)S(1)}, bf16[4,128,128]{2,1,0:T(8,128)(2,1)S(1)}, s32[1]{0:T(128)}) custom-call(s32[4,8]{1,0:T(4,128)S(1)} %copy-done.1, s32[4]{0:T(128)S(1)} %copy-done, bf16[2,4,32]{2,1,0:T(4,128)(2,1)} %screened_ref.1, ...), custom_call_target="tpu_custom_call" | custom-call | flops 6442450944 | bytes 12582912 | tf_op jit(solution)/shard_map/pallas_call | solution.py:307
  17.6 0.0 collective-permute-done.70
  17.6 1.1 %collective-permute-done.71 = bf16[2,2,1,256,256]{4,3,2,1,0:T(8,128)(2,1)S(1)} collective-permute-done((bf16[2,2,1,256,256]{4,3,2,1,0:T(8,128)(2,1)S(1)}, bf16[2,2,1,256,256]{4,3,2,1,0:T(8,128)(2,1)S(1)}, u32[]{:S(2)}, u32[]{:S(2)}) %collective-permute-start.71) | collective-permute-done | bytes 524320 | tf_op jit(solution)/shard_map/ppermute | solution.py:493
  18.7 31.8 %conditional.1 = (bf16[2,2,4,8,4096]{4,3,2,1,0:T(8,128)(2,1)}) conditional(s32[]{:T(128)} %bitcast, (s32[4,8]{1,0:T(4,128)S(1)}, s32[4]{0:T(128)S(1)}, f32[2,2,512,512]{3,2,1,0:T(8,128)S(1)}, bf16[2,2,2,256,256]{4,3,2,1,0:T(8,128)(2,1)S(1)}, bf16[2,2,1,256,256]{4,3,2,1,0:T(8,128)(2,1)S(1)}, ...), branch_computations={%region_0.1_spmd, %region_1.2_spmd, %region_2.3_spmd, %region_3.4_... | conditional | flops 1610612736 | bytes 10486328 | solution.py:508
  18.7 2.8 %branch_2_fun.3 = (bf16[24,16,128]{2,1,0:T(8,128)(2,1)S(1)}, bf16[24,16,128]{2,1,0:T(8,128)(2,1)S(1)}, bf16[24,16,128]{2,1,0:T(8,128)(2,1)S(1)}, bf16[24,16,128]...) custom-call(s32[4,8]{1,0:T(4,128)S(1)} %get-tuple-element.141.kept_r, ...), custom_call_target="tpu_custom_call" | custom-call | flops 1610612736 | bytes 3145728 | tf_op jit(solution)/shard_map/cond/branch_2_fun/pallas_call | solution.py:339
  21.5 2.2 %collective-permute-start.28 = (bf16[24,16,128]{2,1,0:T(8,128)(2,1)S(1)}, bf16[24,16,128]{2,1,0:T(8,128)(2,1)S(1)}, u32[]{:S(2)}, u32[]{:S(2)}) collective-permute-start(bf16[24,16,128]{2,1,0:T(8,128)(2,1)S(1)} %get-tuple-element.148), channel_id=1, source_target_pairs={{0,24},{4,28},{8,16},{12,20},{16,8},{20,12},{24,0},{28,4},{1,25},{... | collective-permute-start | bytes 294920 | tf_op jit(solution)/shard_map/cond/branch_2_fun/ppermute | solution.py:41
  23.7 2.2 %collective-permute-start.29 = (bf16[24,16,128]{2,1,0:T(8,128)(2,1)S(1)}, bf16[24,16,128]{2,1,0:T(8,128)(2,1)S(1)}, u32[]{:S(2)}, u32[]{:S(2)}) collective-permute-start(bf16[24,16,128]{2,1,0:T(8,128)(2,1)S(1)} %get-tuple-element.149), channel_id=1, source_target_pairs={{0,28},{4,24},{8,20},{12,16},{16,12},{20,8},{24,4},{28,0},{1,29},{... | collective-permute-start | bytes 294920 | tf_op jit(solution)/shard_map/cond/branch_2_fun/ppermute | solution.py:41
  26.0 1.2 %collective-permute-start.30 = (bf16[24,16,128]{2,1,0:T(8,128)(2,1)S(1)}, bf16[24,16,128]{2,1,0:T(8,128)(2,1)S(1)}, u32[]{:S(2)}, u32[]{:S(2)}) collective-permute-start(bf16[24,16,128]{2,1,0:T(8,128)(2,1)S(1)} %get-tuple-element.150), channel_id=1, source_target_pairs={{0,8},{4,12},{8,0},{12,4},{16,24},{20,28},{24,16},{28,20},{1,9},{5... | collective-permute-start | bytes 294920 | tf_op jit(solution)/shard_map/cond/branch_2_fun/ppermute | solution.py:41
  27.2 1.2 %collective-permute-start.31 = (bf16[24,16,128]{2,1,0:T(8,128)(2,1)S(1)}, bf16[24,16,128]{2,1,0:T(8,128)(2,1)S(1)}, u32[]{:S(2)}, u32[]{:S(2)}) collective-permute-start(bf16[24,16,128]{2,1,0:T(8,128)(2,1)S(1)} %get-tuple-element.151), channel_id=1, source_target_pairs={{0,16},{4,20},{8,24},{12,28},{16,0},{20,4},{24,8},{28,12},{1,17},{... | collective-permute-start | bytes 294920 | tf_op jit(solution)/shard_map/cond/branch_2_fun/ppermute | solution.py:41
  28.4 0.0 collective-permute-start.32
  28.4 0.0 collective-permute-done.28.refs_1_
  28.4 1.9 %collective-permute-start.33 = (bf16[24,16,128]{2,1,0:T(8,128)(2,1)S(1)}, bf16[24,16,128]{2,1,0:T(8,128)(2,1)S(1)}, u32[]{:S(2)}, u32[]{:S(2)}) collective-permute-start(bf16[24,16,128]{2,1,0:T(8,128)(2,1)S(1)} %get-tuple-element.153), channel_id=1, source_target_pairs={{0,20},{4,16},{8,28},{12,24},{16,4},{20,0},{24,12},{28,8},{1,21},{... | collective-permute-start | bytes 294920 | tf_op jit(solution)/shard_map/cond/branch_2_fun/ppermute | solution.py:41
  30.3 0.0 collective-permute-done.29.refs_2_
  30.3 1.6 %collective-permute-start.34 = (bf16[24,16,128]{2,1,0:T(8,128)(2,1)S(1)}, bf16[24,16,128]{2,1,0:T(8,128)(2,1)S(1)}, u32[]{:S(2)}, u32[]{:S(2)}) collective-permute-start(bf16[24,16,128]{2,1,0:T(8,128)(2,1)S(1)} %get-tuple-element.154), channel_id=1, source_target_pairs={{0,4},{4,0},{8,12},{12,8},{16,20},{20,16},{24,28},{28,24},{1,5},{5... | collective-permute-start | bytes 294920 | tf_op jit(solution)/shard_map/cond/branch_2_fun/ppermute | solution.py:41
  31.9 0.7 %collective-permute-done.30.refs_3_ = bf16[24,16,128]{2,1,0:T(8,128)(2,1)S(1)} collective-permute-done((bf16[24,16,128]{2,1,0:T(8,128)(2,1)S(1)}, bf16[24,16,128]{2,1,0:T(8,128)(2,1)S(1)}, u32[]{:S(2)}, u32[]{:S(2)}) %collective-permute-start.30) | collective-permute-done | bytes 98336 | tf_op jit(solution)/shard_map/cond/branch_2_fun/ppermute | solution.py:41
  32.6 0.2 collective-permute-done.31.refs_4_
  32.8 2.1 %collective-permute-done.32.refs_5_ = bf16[24,16,128]{2,1,0:T(8,128)(2,1)S(1)} collective-permute-done((bf16[24,16,128]{2,1,0:T(8,128)(2,1)S(1)}, bf16[24,16,128]{2,1,0:T(8,128)(2,1)S(1)}, u32[]{:S(2)}, u32[]{:S(2)}) %collective-permute-start.32) | collective-permute-done | bytes 98336 | tf_op jit(solution)/shard_map/cond/branch_2_fun/ppermute | solution.py:41
  34.9 0.0 collective-permute-done.33.refs_6_
  34.9 0.0 collective-permute-done.34.refs_7_
  34.9 1.0 %branch_2_fun.4 = (bf16[24,16,128]{2,1,0:T(8,128)(2,1)S(1)}, bf16[24,16,128]{2,1,0:T(8,128)(2,1)S(1)}, bf16[24,16,128]{2,1,0:T(8,128)(2,1)S(1)}, bf16[24,16,128]...) custom-call(s32[4]{0:T(128)S(1)} %get-tuple-element.139.count_ref, ...), custom_call_target="tpu_custom_call" | custom-call | tf_op jit(solution)/shard_map/cond/branch_2_fun/pallas_call | solution.py:423
  35.9 2.1 %collective-permute-start.35 = (bf16[24,16,128]{2,1,0:T(8,128)(2,1)S(1)}, bf16[24,16,128]{2,1,0:T(8,128)(2,1)S(1)}, u32[]{:S(2)}, u32[]{:S(2)}) collective-permute-start(bf16[24,16,128]{2,1,0:T(8,128)(2,1)S(1)} %get-tuple-element.156), channel_id=1, source_target_pairs={{0,24},{4,28},{8,16},{12,20},{16,8},{20,12},{24,0},{28,4},{1,25},{... | collective-permute-start | bytes 294920 | tf_op jit(solution)/shard_map/cond/branch_2_fun/ppermute | solution.py:41
  38.0 0.9 %collective-permute-start.36 = (bf16[24,16,128]{2,1,0:T(8,128)(2,1)S(1)}, bf16[24,16,128]{2,1,0:T(8,128)(2,1)S(1)}, u32[]{:S(2)}, u32[]{:S(2)}) collective-permute-start(bf16[24,16,128]{2,1,0:T(8,128)(2,1)S(1)} %get-tuple-element.157), channel_id=1, source_target_pairs={{0,28},{4,24},{8,20},{12,16},{16,12},{20,8},{24,4},{28,0},{1,29},{... | collective-permute-start | bytes 294920 | tf_op jit(solution)/shard_map/cond/branch_2_fun/ppermute | solution.py:41
  38.9 1.2 %collective-permute-start.37 = (bf16[24,16,128]{2,1,0:T(8,128)(2,1)S(1)}, bf16[24,16,128]{2,1,0:T(8,128)(2,1)S(1)}, u32[]{:S(2)}, u32[]{:S(2)}) collective-permute-start(bf16[24,16,128]{2,1,0:T(8,128)(2,1)S(1)} %get-tuple-element.158), channel_id=1, source_target_pairs={{0,8},{4,12},{8,0},{12,4},{16,24},{20,28},{24,16},{28,20},{1,9},{5... | collective-permute-start | bytes 294920 | tf_op jit(solution)/shard_map/cond/branch_2_fun/ppermute | solution.py:41
  40.0 1.2 %collective-permute-start.38 = (bf16[24,16,128]{2,1,0:T(8,128)(2,1)S(1)}, bf16[24,16,128]{2,1,0:T(8,128)(2,1)S(1)}, u32[]{:S(2)}, u32[]{:S(2)}) collective-permute-start(bf16[24,16,128]{2,1,0:T(8,128)(2,1)S(1)} %get-tuple-element.159), channel_id=1, source_target_pairs={{0,16},{4,20},{8,24},{12,28},{16,0},{20,4},{24,8},{28,12},{1,17},{... | collective-permute-start | bytes 294920 | tf_op jit(solution)/shard_map/cond/branch_2_fun/ppermute | solution.py:41
  41.3 0.5 %collective-permute-start.39 = (bf16[24,16,128]{2,1,0:T(8,128)(2,1)S(1)}, bf16[24,16,128]{2,1,0:T(8,128)(2,1)S(1)}, u32[]{:S(2)}, u32[]{:S(2)}) collective-permute-start(bf16[24,16,128]{2,1,0:T(8,128)(2,1)S(1)} %get-tuple-element.160), channel_id=1, source_target_pairs={{0,12},{4,8},{8,4},{12,0},{16,28},{20,24},{24,20},{28,16},{1,13},{... | collective-permute-start | bytes 294920 | tf_op jit(solution)/shard_map/cond/branch_2_fun/ppermute | solution.py:41
  41.8 0.0 collective-permute-done.35.refs_1_
  41.8 1.7 %collective-permute-start.40 = (bf16[24,16,128]{2,1,0:T(8,128)(2,1)S(1)}, bf16[24,16,128]{2,1,0:T(8,128)(2,1)S(1)}, u32[]{:S(2)}, u32[]{:S(2)}) collective-permute-start(bf16[24,16,128]{2,1,0:T(8,128)(2,1)S(1)} %get-tuple-element.161), channel_id=1, source_target_pairs={{0,20},{4,16},{8,28},{12,24},{16,4},{20,0},{24,12},{28,8},{1,21},{... | collective-permute-start | bytes 294920 | tf_op jit(solution)/shard_map/cond/branch_2_fun/ppermute | solution.py:41
  43.5 0.8 %collective-permute-done.36.refs_2_ = bf16[24,16,128]{2,1,0:T(8,128)(2,1)S(1)} collective-permute-done((bf16[24,16,128]{2,1,0:T(8,128)(2,1)S(1)}, bf16[24,16,128]{2,1,0:T(8,128)(2,1)S(1)}, u32[]{:S(2)}, u32[]{:S(2)}) %collective-permute-start.36) | collective-permute-done | bytes 98336 | tf_op jit(solution)/shard_map/cond/branch_2_fun/ppermute | solution.py:41
  44.3 0.5 %collective-permute-start.41 = (bf16[24,16,128]{2,1,0:T(8,128)(2,1)S(1)}, bf16[24,16,128]{2,1,0:T(8,128)(2,1)S(1)}, u32[]{:S(2)}, u32[]{:S(2)}) collective-permute-start(bf16[24,16,128]{2,1,0:T(8,128)(2,1)S(1)} %get-tuple-element.162), channel_id=1, source_target_pairs={{0,4},{4,0},{8,12},{12,8},{16,20},{20,16},{24,28},{28,24},{1,5},{5... | collective-permute-start | bytes 294920 | tf_op jit(solution)/shard_map/cond/branch_2_fun/ppermute | solution.py:41
  44.8 0.7 %collective-permute-done.37.refs_3_ = bf16[24,16,128]{2,1,0:T(8,128)(2,1)S(1)} collective-permute-done((bf16[24,16,128]{2,1,0:T(8,128)(2,1)S(1)}, bf16[24,16,128]{2,1,0:T(8,128)(2,1)S(1)}, u32[]{:S(2)}, u32[]{:S(2)}) %collective-permute-start.37) | collective-permute-done | bytes 98336 | tf_op jit(solution)/shard_map/cond/branch_2_fun/ppermute | solution.py:41
  45.5 0.9 %collective-permute-done.38.refs_4_ = bf16[24,16,128]{2,1,0:T(8,128)(2,1)S(1)} collective-permute-done((bf16[24,16,128]{2,1,0:T(8,128)(2,1)S(1)}, bf16[24,16,128]{2,1,0:T(8,128)(2,1)S(1)}, u32[]{:S(2)}, u32[]{:S(2)}) %collective-permute-start.38) | collective-permute-done | bytes 98336 | tf_op jit(solution)/shard_map/cond/branch_2_fun/ppermute | solution.py:41
  46.4 1.6 %collective-permute-done.39.refs_5_ = bf16[24,16,128]{2,1,0:T(8,128)(2,1)S(1)} collective-permute-done((bf16[24,16,128]{2,1,0:T(8,128)(2,1)S(1)}, bf16[24,16,128]{2,1,0:T(8,128)(2,1)S(1)}, u32[]{:S(2)}, u32[]{:S(2)}) %collective-permute-start.39) | collective-permute-done | bytes 98336 | tf_op jit(solution)/shard_map/cond/branch_2_fun/ppermute | solution.py:41
  48.0 0.5 collective-permute-done.40.refs_6_
  48.5 0.0 collective-permute-done.41.refs_7_
  48.5 1.6 %branch_2_fun.5 = bf16[2,2,4,8,4096]{4,3,2,1,0:T(8,128)(2,1)} custom-call(s32[4]{0:T(128)S(1)} %get-tuple-element.139.count_ref, bf16[24,16,128]{2,1,0:T(8,128)(2,1)S(1)} %get-tuple-element.155.refs_0_, bf16[24,16,128]{2,1,0:T(8,128)(2,1)S(1)} %collective-permute-done.35.refs_1_, bf16[24,16,128]{2,1,0:T(8,128)(2,1)S(1)} %collective-permute-done.36.refs_2_, ...), custom_call_target="tpu_custom_call" | custom-call | tf_op jit(solution)/shard_map/cond/branch_2_fun/pallas_call | solution.py:471
Async XLA Ops:
  0.0 6.3 %copy-start = (s32[4]{0:T(128)S(1)}, s32[4]{0:T(128)}, u32[]{:S(2)}) copy-start(s32[4]{0:T(128)} %count_ref.1) | copy-start | bytes 52
  0.0 6.3 %copy-start.1 = (s32[4,8]{1,0:T(4,128)S(1)}, s32[4,8]{1,0:T(4,128)}, u32[]{:S(2)}) copy-start(s32[4,8]{1,0:T(4,128)} %kept_ref.1) | copy-start | bytes 388
  1.9 15.7 %collective-permute-start.70 = (bf16[2,2,1,256,256]{4,3,2,1,0:T(8,128)(2,1)}, bf16[2,2,1,256,256]{4,3,2,1,0:T(8,128)(2,1)S(1)}, u32[]{:S(2)}, u32[]{:S(2)}) collective-permute-start(bf16[2,2,1,256,256]{4,3,2,1,0:T(8,128)(2,1)} %shard_map.79), channel_id=1, source_target_pairs={{0,1},{2,3},{1,0},{3,2},{4,5},{6,7},{5,4},{7,6},{8,9},{10,11},{9,8... | collective-permute-start | bytes 1572872 | tf_op jit(solution)/shard_map/ppermute | solution.py:493
  4.3 14.4 %collective-permute-start.71 = (bf16[2,2,1,256,256]{4,3,2,1,0:T(8,128)(2,1)S(1)}, bf16[2,2,1,256,256]{4,3,2,1,0:T(8,128)(2,1)S(1)}, u32[]{:S(2)}, u32[]{:S(2)}) collective-permute-start(bf16[2,2,1,256,256]{4,3,2,1,0:T(8,128)(2,1)S(1)} %constant_dynamic-slice_fusion), channel_id=1, source_target_pairs={{1,2},{2,1},{5,6},{6,5},{9,10},{10,9},{13,14},{14,13},{17,18},{18,... | collective-permute-start | bytes 1572872 | tf_op jit(solution)/shard_map/ppermute | solution.py:493
  21.5 6.9 %collective-permute-start.28 = (bf16[24,16,128]{2,1,0:T(8,128)(2,1)S(1)}, bf16[24,16,128]{2,1,0:T(8,128)(2,1)S(1)}, u32[]{:S(2)}, u32[]{:S(2)}) collective-permute-start(bf16[24,16,128]{2,1,0:T(8,128)(2,1)S(1)} %get-tuple-element.148), channel_id=1, source_target_pairs={{0,24},{4,28},{8,16},{12,20},{16,8},{20,12},{24,0},{28,4},{1,25},{... | collective-permute-start | bytes 294920 | tf_op jit(solution)/shard_map/cond/branch_2_fun/ppermute | solution.py:41
  23.7 6.5 %collective-permute-start.29 = (bf16[24,16,128]{2,1,0:T(8,128)(2,1)S(1)}, bf16[24,16,128]{2,1,0:T(8,128)(2,1)S(1)}, u32[]{:S(2)}, u32[]{:S(2)}) collective-permute-start(bf16[24,16,128]{2,1,0:T(8,128)(2,1)S(1)} %get-tuple-element.149), channel_id=1, source_target_pairs={{0,28},{4,24},{8,20},{12,16},{16,12},{20,8},{24,4},{28,0},{1,29},{... | collective-permute-start | bytes 294920 | tf_op jit(solution)/shard_map/cond/branch_2_fun/ppermute | solution.py:41
  26.0 6.6 %collective-permute-start.30 = (bf16[24,16,128]{2,1,0:T(8,128)(2,1)S(1)}, bf16[24,16,128]{2,1,0:T(8,128)(2,1)S(1)}, u32[]{:S(2)}, u32[]{:S(2)}) collective-permute-start(bf16[24,16,128]{2,1,0:T(8,128)(2,1)S(1)} %get-tuple-element.150), channel_id=1, source_target_pairs={{0,8},{4,12},{8,0},{12,4},{16,24},{20,28},{24,16},{28,20},{1,9},{5... | collective-permute-start | bytes 294920 | tf_op jit(solution)/shard_map/cond/branch_2_fun/ppermute | solution.py:41
  27.2 5.6 %collective-permute-start.31 = (bf16[24,16,128]{2,1,0:T(8,128)(2,1)S(1)}, bf16[24,16,128]{2,1,0:T(8,128)(2,1)S(1)}, u32[]{:S(2)}, u32[]{:S(2)}) collective-permute-start(bf16[24,16,128]{2,1,0:T(8,128)(2,1)S(1)} %get-tuple-element.151), channel_id=1, source_target_pairs={{0,16},{4,20},{8,24},{12,28},{16,0},{20,4},{24,8},{28,12},{1,17},{... | collective-permute-start | bytes 294920 | tf_op jit(solution)/shard_map/cond/branch_2_fun/ppermute | solution.py:41
  28.4 6.5 %collective-permute-start.32 = (bf16[24,16,128]{2,1,0:T(8,128)(2,1)S(1)}, bf16[24,16,128]{2,1,0:T(8,128)(2,1)S(1)}, u32[]{:S(2)}, u32[]{:S(2)}) collective-permute-start(bf16[24,16,128]{2,1,0:T(8,128)(2,1)S(1)} %get-tuple-element.152), channel_id=1, source_target_pairs={{0,12},{4,8},{8,4},{12,0},{16,28},{20,24},{24,20},{28,16},{1,13},{... | collective-permute-start | bytes 294920 | tf_op jit(solution)/shard_map/cond/branch_2_fun/ppermute | solution.py:41
  28.4 6.5 %collective-permute-start.33 = (bf16[24,16,128]{2,1,0:T(8,128)(2,1)S(1)}, bf16[24,16,128]{2,1,0:T(8,128)(2,1)S(1)}, u32[]{:S(2)}, u32[]{:S(2)}) collective-permute-start(bf16[24,16,128]{2,1,0:T(8,128)(2,1)S(1)} %get-tuple-element.153), channel_id=1, source_target_pairs={{0,20},{4,16},{8,28},{12,24},{16,4},{20,0},{24,12},{28,8},{1,21},{... | collective-permute-start | bytes 294920 | tf_op jit(solution)/shard_map/cond/branch_2_fun/ppermute | solution.py:41
  30.3 4.6 %collective-permute-start.34 = (bf16[24,16,128]{2,1,0:T(8,128)(2,1)S(1)}, bf16[24,16,128]{2,1,0:T(8,128)(2,1)S(1)}, u32[]{:S(2)}, u32[]{:S(2)}) collective-permute-start(bf16[24,16,128]{2,1,0:T(8,128)(2,1)S(1)} %get-tuple-element.154), channel_id=1, source_target_pairs={{0,4},{4,0},{8,12},{12,8},{16,20},{20,16},{24,28},{28,24},{1,5},{5... | collective-permute-start | bytes 294920 | tf_op jit(solution)/shard_map/cond/branch_2_fun/ppermute | solution.py:41
  35.9 5.9 %collective-permute-start.35 = (bf16[24,16,128]{2,1,0:T(8,128)(2,1)S(1)}, bf16[24,16,128]{2,1,0:T(8,128)(2,1)S(1)}, u32[]{:S(2)}, u32[]{:S(2)}) collective-permute-start(bf16[24,16,128]{2,1,0:T(8,128)(2,1)S(1)} %get-tuple-element.156), channel_id=1, source_target_pairs={{0,24},{4,28},{8,16},{12,20},{16,8},{20,12},{24,0},{28,4},{1,25},{... | collective-permute-start | bytes 294920 | tf_op jit(solution)/shard_map/cond/branch_2_fun/ppermute | solution.py:41
  38.0 6.3 %collective-permute-start.36 = (bf16[24,16,128]{2,1,0:T(8,128)(2,1)S(1)}, bf16[24,16,128]{2,1,0:T(8,128)(2,1)S(1)}, u32[]{:S(2)}, u32[]{:S(2)}) collective-permute-start(bf16[24,16,128]{2,1,0:T(8,128)(2,1)S(1)} %get-tuple-element.157), channel_id=1, source_target_pairs={{0,28},{4,24},{8,20},{12,16},{16,12},{20,8},{24,4},{28,0},{1,29},{... | collective-permute-start | bytes 294920 | tf_op jit(solution)/shard_map/cond/branch_2_fun/ppermute | solution.py:41
  38.9 6.6 %collective-permute-start.37 = (bf16[24,16,128]{2,1,0:T(8,128)(2,1)S(1)}, bf16[24,16,128]{2,1,0:T(8,128)(2,1)S(1)}, u32[]{:S(2)}, u32[]{:S(2)}) collective-permute-start(bf16[24,16,128]{2,1,0:T(8,128)(2,1)S(1)} %get-tuple-element.158), channel_id=1, source_target_pairs={{0,8},{4,12},{8,0},{12,4},{16,24},{20,28},{24,16},{28,20},{1,9},{5... | collective-permute-start | bytes 294920 | tf_op jit(solution)/shard_map/cond/branch_2_fun/ppermute | solution.py:41
  40.0 6.3 %collective-permute-start.38 = (bf16[24,16,128]{2,1,0:T(8,128)(2,1)S(1)}, bf16[24,16,128]{2,1,0:T(8,128)(2,1)S(1)}, u32[]{:S(2)}, u32[]{:S(2)}) collective-permute-start(bf16[24,16,128]{2,1,0:T(8,128)(2,1)S(1)} %get-tuple-element.159), channel_id=1, source_target_pairs={{0,16},{4,20},{8,24},{12,28},{16,0},{20,4},{24,8},{28,12},{1,17},{... | collective-permute-start | bytes 294920 | tf_op jit(solution)/shard_map/cond/branch_2_fun/ppermute | solution.py:41
  41.3 6.7 %collective-permute-start.39 = (bf16[24,16,128]{2,1,0:T(8,128)(2,1)S(1)}, bf16[24,16,128]{2,1,0:T(8,128)(2,1)S(1)}, u32[]{:S(2)}, u32[]{:S(2)}) collective-permute-start(bf16[24,16,128]{2,1,0:T(8,128)(2,1)S(1)} %get-tuple-element.160), channel_id=1, source_target_pairs={{0,12},{4,8},{8,4},{12,0},{16,28},{20,24},{24,20},{28,16},{1,13},{... | collective-permute-start | bytes 294920 | tf_op jit(solution)/shard_map/cond/branch_2_fun/ppermute | solution.py:41
  41.8 6.7 %collective-permute-start.40 = (bf16[24,16,128]{2,1,0:T(8,128)(2,1)S(1)}, bf16[24,16,128]{2,1,0:T(8,128)(2,1)S(1)}, u32[]{:S(2)}, u32[]{:S(2)}) collective-permute-start(bf16[24,16,128]{2,1,0:T(8,128)(2,1)S(1)} %get-tuple-element.161), channel_id=1, source_target_pairs={{0,20},{4,16},{8,28},{12,24},{16,4},{20,0},{24,12},{28,8},{1,21},{... | collective-permute-start | bytes 294920 | tf_op jit(solution)/shard_map/cond/branch_2_fun/ppermute | solution.py:41
  44.3 4.2 %collective-permute-start.41 = (bf16[24,16,128]{2,1,0:T(8,128)(2,1)S(1)}, bf16[24,16,128]{2,1,0:T(8,128)(2,1)S(1)}, u32[]{:S(2)}, u32[]{:S(2)}) collective-permute-start(bf16[24,16,128]{2,1,0:T(8,128)(2,1)S(1)} %get-tuple-element.162), channel_id=1, source_target_pairs={{0,4},{4,0},{8,12},{12,8},{16,20},{20,16},{24,28},{28,24},{1,5},{5... | collective-permute-start | bytes 294920 | tf_op jit(solution)/shard_map/cond/branch_2_fun/ppermute | solution.py:41
where the time goes:
time: 50 us; the launch traced here: 50.7 us
  starting transfers between devices  21.8 us (44%)
  Pallas kernels  18 us (36%)
  waiting for transfers between devices  8.48 us (17%)
  local copies, waits for them, and re-layouts  1.08 us (2%)
  between operations  0.85 us (2%)
    ppermute x14, starting transfers between devices, exchange(): lax.ppermute(part, 'energy', [(source, source ^ bits) for source in range...  18.5 us
    pallas_call x1, Pallas kernels, local_part(): pl.pallas_call(partial(local_kernel, packing_order(cells), devices, sizes...  10.7 us
    ppermute x14, waiting for transfers between devices, exchange(): lax.ppermute(part, 'energy', [(source, source ^ bits) for source in range...  7.39 us
    ppermute x2, starting transfers between devices, swap(): lax.ppermute(block, 'cell', pairs + [(high, low) for low, high in pairs])  3.28 us
    pallas_call x1, Pallas kernels, edges(): pl.pallas_call(partial(edge_kernel, packing_order(kept.shape[0])), in_spe...  2.8 us
    pallas_call x1, Pallas kernels, border(): pl.pallas_call(border_kernel, in_specs=[STAYING], out_specs=VECTORS, out_...  1.87 us
    pallas_call x1, Pallas kernels, unpack(): pl.pallas_call(partial(unpack_kernel, packing_order(cells)), in_specs=[SC...  1.63 us
    ppermute x2, waiting for transfers between devices, swap(): lax.ppermute(block, 'cell', pairs + [(high, low) for low, high in pairs])  1.09 us
  transfers between devices with their start and end apart: 16, of which 9 were waited for; matrix products, arithmetic and copies ran while one was open for 2% of the time, Pallas kernels for 21%

commit v1 on v0

--- a/solution.py
+++ b/solution.py
@@ -349,24 +349,6 @@
         compiler_params=pltpu.CompilerParams(vmem_limit_bytes=32 << 20),
         cost_estimate=cost_of(1, energies, size),
     )(kept, kept_count, partial_sum, outer, *halo, earlier)
-
-
-def border_kernel(sigma, out, sem):
-    cell = jnp.where(lax.axis_index("cell") % 2 == 1, 0, sigma.shape[2] - 1)
-    copy = pltpu.make_async_copy(sigma.at[:, :, pl.ds(cell, 1)], out, sem)
-    copy.start()
-    copy.wait()
-
-
-def border(sigma):
-    return pl.pallas_call(
-        border_kernel,
-        in_specs=[STAYING],
-        out_specs=VECTORS,
-        out_shape=jax.ShapeDtypeStruct(sigma.shape[:2] + (1,) + sigma.shape[3:], sigma.dtype),
-        scratch_shapes=[pltpu.SemaphoreType.DMA],
-        compiler_params=pltpu.CompilerParams(vmem_limit_bytes=60 << 20),
-    )(sigma)
 
 
 def fill_mixing(screened_ref, weight_ref, table):
@@ -485,14 +467,14 @@
 def per_device(diag, lower, upper, sigma, screened, kept, kept_count):
     count = lax.axis_size("cell")
     devices = lax.axis_size("energy")
-    outward = lax.axis_index("cell") % 2 * (sigma.shape[2] - 1)
-    edge_cell = lax.dynamic_slice_in_dim(sigma, outward, 1, axis=2)
+    odd = lax.axis_index("cell") % 2 == 1
+    first, last = sigma[:, :, :1], sigma[:, :, -1:]
 
     def swap(block, start):
         pairs = [(low, low + 1) for low in range(start, count - 1, 2)]
         return lax.ppermute(block, "cell", pairs + [(high, low) for low, high in pairs])
 
-    halo = swap(border(sigma), 0), swap(edge_cell, 1)
+    halo = swap(jnp.where(odd, first, last), 0), swap(jnp.where(odd, last, first), 1)
     energies, slots = sigma.shape[1], kept.shape[1]
     full = kept.shape[0] * slots
     sizes = [full * eighths // 8 for eighths in (4, 5, 6, 7, 8)]

time: 50 us -> 46.7 us (0.934)
  the two profiles are of different devices: /device:TPU:17 before, /device:TPU:0 now
where the time goes in v1:
time: 46.7 us; the launch traced here: 47 us
  starting transfers between devices  18.9 us (40%)
  Pallas kernels  16.1 us (34%)
  waiting for transfers between devices  9.63 us (21%)
  other arithmetic  1.3 us (3%)
  between operations  0.86 us (2%)
    ppermute x14, starting transfers between devices, exchange(): lax.ppermute(part, 'energy', [(source, source ^ bits) for source in range...  12.3 us
    pallas_call x1, Pallas kernels, local_part(): pl.pallas_call(partial(local_kernel, packing_order(cells), devices, sizes...  10.7 us
    ppermute x14, waiting for transfers between devices, exchange(): lax.ppermute(part, 'energy', [(source, source ^ bits) for source in range...  9.34 us
    ppermute x2, starting transfers between devices, swap(): lax.ppermute(block, 'cell', pairs + [(high, low) for low, high in pairs])  6.57 us
    pallas_call x1, Pallas kernels, edges(): pl.pallas_call(partial(edge_kernel, packing_order(kept.shape[0])), in_spe...  2.79 us
    pallas_call x1, Pallas kernels, unpack(): pl.pallas_call(partial(unpack_kernel, packing_order(cells)), in_specs=[SC...  1.63 us
    select_n x1, other arithmetic, per_device(): jnp.where(odd, last, first)  1.3 us
    pallas_call x1, Pallas kernels, mix(): pl.pallas_call(partial(mix_kernel, packing_order(kept_count.shape[0])), i...  0.97 us
  transfers between devices with their start and end apart: 16, of which 9 were waited for; matrix products, arithmetic and copies ran while one was open for 0% of the time, Pallas kernels for 23%

profile of v1, /device:TPU:0, one launch (start us, length us, event | category | flops | bytes accessed | tf_op | source)
XLA Modules:
  0.0 47.0 jit_solution(16605430518782644197)
XLA Ops:
  0.0 0.0 copy-start
  0.0 0.0 copy-start.1
  0.0 1.3 %broadcast_select_fusion = (bf16[2,2,1,256,256]{4,3,2,1,0:T(8,128)(2,1)S(1)}, bf16[2,2,1,256,256]{4,3,2,1,0:T(8,128)(2,1)S(1)}) fusion(pred[]{:T(512)S(6)} %eq.5, bf16[2,2,4,256,256]{4,3,2,1,0:T(8,128)(2,1)} %refs_3_.1), kind=kLoop, calls=%fused_computation | loop fusion | flops 524288 | bytes 2097153 | tf_op jit(solution)/shard_map/jit(_where)/select_n | solution.py:477
  1.3 0.7 %collective-permute-start.71 = (bf16[2,2,1,256,256]{4,3,2,1,0:T(8,128)(2,1)S(1)}, bf16[2,2,1,256,256]{4,3,2,1,0:T(8,128)(2,1)S(1)}, u32[]{:S(2)}, u32[]{:S(2)}) collective-permute-start(bf16[2,2,1,256,256]{4,3,2,1,0:T(8,128)(2,1)S(1)} %get-tuple-element.222), channel_id=1, source_target_pairs={{1,2},{2,1},{5,6},{6,5},{9,10},{10,9},{13,14},{14,13},{17,18},{18,... | collective-permute-start | bytes 1572872 | tf_op jit(solution)/shard_map/ppermute | solution.py:475
  2.0 5.9 %collective-permute-start.70 = (bf16[2,2,1,256,256]{4,3,2,1,0:T(8,128)(2,1)S(1)}, bf16[2,2,1,256,256]{4,3,2,1,0:T(8,128)(2,1)S(1)}, u32[]{:S(2)}, u32[]{:S(2)}) collective-permute-start(bf16[2,2,1,256,256]{4,3,2,1,0:T(8,128)(2,1)S(1)} %get-tuple-element.223), channel_id=1, source_target_pairs={{0,1},{2,3},{1,0},{3,2},{4,5},{6,7},{5,4},{7,6},{8,9},{10,11},{9,8... | collective-permute-start | bytes 1572872 | tf_op jit(solution)/shard_map/ppermute | solution.py:475
  7.9 0.0 copy-done
  7.9 0.0 copy-done.1
  7.9 10.7 %shard_map.78 = (bf16[8,16,16,128]{3,2,1,0:T(8,128)(2,1)S(1)}, f32[2,2,512,512]{3,2,1,0:T(8,128)S(1)}, bf16[2,2,2,256,256]{4,3,2,1,0:T(8,128)(2,1)S(1)}, bf16[4,128,128]{2,1,0:T(8,128)(2,1)S(1)}, s32[1]{0:T(128)}) custom-call(s32[4,8]{1,0:T(4,128)S(1)} %copy-done.1, s32[4]{0:T(128)S(1)} %copy-done, bf16[2,4,32]{2,1,0:T(4,128)(2,1)} %screened_ref.1, ...), custom_call_target="tpu_custom_call" | custom-call | flops 6442450944 | bytes 12582912 | tf_op jit(solution)/shard_map/pallas_call | solution.py:307
  19.2 0.0 collective-permute-done.71
  19.2 0.3 collective-permute-done.70
  19.5 27.3 %conditional.1 = (bf16[2,2,4,8,4096]{4,3,2,1,0:T(8,128)(2,1)}) conditional(s32[]{:T(128)} %bitcast, (s32[4,8]{1,0:T(4,128)S(1)}, s32[4]{0:T(128)S(1)}, f32[2,2,512,512]{3,2,1,0:T(8,128)S(1)}, bf16[2,2,2,256,256]{4,3,2,1,0:T(8,128)(2,1)S(1)}, bf16[2,2,1,256,256]{4,3,2,1,0:T(8,128)(2,1)S(1)}, ...), branch_computations={%region_0.1_spmd, %region_1.2_spmd, %region_2.3_spmd, %region_3.4_... | conditional | flops 1610612736 | bytes 10486328 | solution.py:490
  19.5 2.8 %branch_1_fun.3 = (bf16[20,16,128]{2,1,0:T(8,128)(2,1)S(1)}, bf16[20,16,128]{2,1,0:T(8,128)(2,1)S(1)}, bf16[20,16,128]{2,1,0:T(8,128)(2,1)S(1)}, bf16[20,16,128]...) custom-call(s32[4,8]{1,0:T(4,128)S(1)} %get-tuple-element.117.kept_r, ...), custom_call_target="tpu_custom_call" | custom-call | flops 1610612736 | bytes 3145728 | tf_op jit(solution)/shard_map/cond/branch_1_fun/pallas_call | solution.py:339
  22.3 2.5 %collective-permute-start.14 = (bf16[20,16,128]{2,1,0:T(8,128)(2,1)S(1)}, bf16[20,16,128]{2,1,0:T(8,128)(2,1)S(1)}, u32[]{:S(2)}, u32[]{:S(2)}) collective-permute-start(bf16[20,16,128]{2,1,0:T(8,128)(2,1)S(1)} %get-tuple-element.124), channel_id=1, source_target_pairs={{0,24},{4,28},{8,16},{12,20},{16,8},{20,12},{24,0},{28,4},{1,25},{... | collective-permute-start | bytes 245768 | tf_op jit(solution)/shard_map/cond/branch_1_fun/ppermute | solution.py:41
  24.8 0.0 collective-permute-start.15
  24.8 0.5 %collective-permute-start.16 = (bf16[20,16,128]{2,1,0:T(8,128)(2,1)S(1)}, bf16[20,16,128]{2,1,0:T(8,128)(2,1)S(1)}, u32[]{:S(2)}, u32[]{:S(2)}) collective-permute-start(bf16[20,16,128]{2,1,0:T(8,128)(2,1)S(1)} %get-tuple-element.126), channel_id=1, source_target_pairs={{0,8},{4,12},{8,0},{12,4},{16,24},{20,28},{24,16},{28,20},{1,9},{5... | collective-permute-start | bytes 245768 | tf_op jit(solution)/shard_map/cond/branch_1_fun/ppermute | solution.py:41
  25.4 1.3 %collective-permute-start.17 = (bf16[20,16,128]{2,1,0:T(8,128)(2,1)S(1)}, bf16[20,16,128]{2,1,0:T(8,128)(2,1)S(1)}, u32[]{:S(2)}, u32[]{:S(2)}) collective-permute-start(bf16[20,16,128]{2,1,0:T(8,128)(2,1)S(1)} %get-tuple-element.127), channel_id=1, source_target_pairs={{0,16},{4,20},{8,24},{12,28},{16,0},{20,4},{24,8},{28,12},{1,17},{... | collective-permute-start | bytes 245768 | tf_op jit(solution)/shard_map/cond/branch_1_fun/ppermute | solution.py:41
  26.7 1.3 %collective-permute-start.18 = (bf16[20,16,128]{2,1,0:T(8,128)(2,1)S(1)}, bf16[20,16,128]{2,1,0:T(8,128)(2,1)S(1)}, u32[]{:S(2)}, u32[]{:S(2)}) collective-permute-start(bf16[20,16,128]{2,1,0:T(8,128)(2,1)S(1)} %get-tuple-element.128), channel_id=1, source_target_pairs={{0,12},{4,8},{8,4},{12,0},{16,28},{20,24},{24,20},{28,16},{1,13},{... | collective-permute-start | bytes 245768 | tf_op jit(solution)/shard_map/cond/branch_1_fun/ppermute | solution.py:41
  28.0 0.0 collective-permute-done.14.refs_1_
  28.0 0.6 %collective-permute-start.19 = (bf16[20,16,128]{2,1,0:T(8,128)(2,1)S(1)}, bf16[20,16,128]{2,1,0:T(8,128)(2,1)S(1)}, u32[]{:S(2)}, u32[]{:S(2)}) collective-permute-start(bf16[20,16,128]{2,1,0:T(8,128)(2,1)S(1)} %get-tuple-element.129), channel_id=1, source_target_pairs={{0,20},{4,16},{8,28},{12,24},{16,4},{20,0},{24,12},{28,8},{1,21},{... | collective-permute-start | bytes 245768 | tf_op jit(solution)/shard_map/cond/branch_1_fun/ppermute | solution.py:41
  28.6 1.9 %collective-permute-done.15.refs_2_ = bf16[20,16,128]{2,1,0:T(8,128)(2,1)S(1)} collective-permute-done((bf16[20,16,128]{2,1,0:T(8,128)(2,1)S(1)}, bf16[20,16,128]{2,1,0:T(8,128)(2,1)S(1)}, u32[]{:S(2)}, u32[]{:S(2)}) %collective-permute-start.15) | collective-permute-done | bytes 81952 | tf_op jit(solution)/shard_map/cond/branch_1_fun/ppermute | solution.py:41
  30.5 0.0 collective-permute-start.20
  30.5 0.9 %collective-permute-done.16.refs_3_ = bf16[20,16,128]{2,1,0:T(8,128)(2,1)S(1)} collective-permute-done((bf16[20,16,128]{2,1,0:T(8,128)(2,1)S(1)}, bf16[20,16,128]{2,1,0:T(8,128)(2,1)S(1)}, u32[]{:S(2)}, u32[]{:S(2)}) %collective-permute-start.16) | collective-permute-done | bytes 81952 | tf_op jit(solution)/shard_map/cond/branch_1_fun/ppermute | solution.py:41
  31.3 0.0 collective-permute-done.17.refs_4_
  31.3 1.7 %collective-permute-done.18.refs_5_ = bf16[20,16,128]{2,1,0:T(8,128)(2,1)S(1)} collective-permute-done((bf16[20,16,128]{2,1,0:T(8,128)(2,1)S(1)}, bf16[20,16,128]{2,1,0:T(8,128)(2,1)S(1)}, u32[]{:S(2)}, u32[]{:S(2)}) %collective-permute-start.18) | collective-permute-done | bytes 81952 | tf_op jit(solution)/shard_map/cond/branch_1_fun/ppermute | solution.py:41
  33.0 0.2 collective-permute-done.19.refs_6_
  33.3 0.0 collective-permute-done.20.refs_7_
  33.3 1.0 %branch_1_fun.4 = (bf16[20,16,128]{2,1,0:T(8,128)(2,1)S(1)}, bf16[20,16,128]{2,1,0:T(8,128)(2,1)S(1)}, bf16[20,16,128]{2,1,0:T(8,128)(2,1)S(1)}, bf16[20,16,128]...) custom-call(s32[4]{0:T(128)S(1)} %get-tuple-element.115.count_ref, ...), custom_call_target="tpu_custom_call" | custom-call | tf_op jit(solution)/shard_map/cond/branch_1_fun/pallas_call | solution.py:405
  34.2 2.2 %collective-permute-start.21 = (bf16[20,16,128]{2,1,0:T(8,128)(2,1)S(1)}, bf16[20,16,128]{2,1,0:T(8,128)(2,1)S(1)}, u32[]{:S(2)}, u32[]{:S(2)}) collective-permute-start(bf16[20,16,128]{2,1,0:T(8,128)(2,1)S(1)} %get-tuple-element.132), channel_id=1, source_target_pairs={{0,24},{4,28},{8,16},{12,20},{16,8},{20,12},{24,0},{28,4},{1,25},{... | collective-permute-start | bytes 245768 | tf_op jit(solution)/shard_map/cond/branch_1_fun/ppermute | solution.py:41
  36.4 0.1 collective-permute-start.22
  36.5 1.1 %collective-permute-start.23 = (bf16[20,16,128]{2,1,0:T(8,128)(2,1)S(1)}, bf16[20,16,128]{2,1,0:T(8,128)(2,1)S(1)}, u32[]{:S(2)}, u32[]{:S(2)}) collective-permute-start(bf16[20,16,128]{2,1,0:T(8,128)(2,1)S(1)} %get-tuple-element.134), channel_id=1, source_target_pairs={{0,8},{4,12},{8,0},{12,4},{16,24},{20,28},{24,16},{28,20},{1,9},{5... | collective-permute-start | bytes 245768 | tf_op jit(solution)/shard_map/cond/branch_1_fun/ppermute | solution.py:41
  37.6 1.2 %collective-permute-start.24 = (bf16[20,16,128]{2,1,0:T(8,128)(2,1)S(1)}, bf16[20,16,128]{2,1,0:T(8,128)(2,1)S(1)}, u32[]{:S(2)}, u32[]{:S(2)}) collective-permute-start(bf16[20,16,128]{2,1,0:T(8,128)(2,1)S(1)} %get-tuple-element.135), channel_id=1, source_target_pairs={{0,16},{4,20},{8,24},{12,28},{16,0},{20,4},{24,8},{28,12},{1,17},{... | collective-permute-start | bytes 245768 | tf_op jit(solution)/shard_map/cond/branch_1_fun/ppermute | solution.py:41
  38.8 0.9 %collective-permute-start.25 = (bf16[20,16,128]{2,1,0:T(8,128)(2,1)S(1)}, bf16[20,16,128]{2,1,0:T(8,128)(2,1)S(1)}, u32[]{:S(2)}, u32[]{:S(2)}) collective-permute-start(bf16[20,16,128]{2,1,0:T(8,128)(2,1)S(1)} %get-tuple-element.136), channel_id=1, source_target_pairs={{0,12},{4,8},{8,4},{12,0},{16,28},{20,24},{24,20},{28,16},{1,13},{... | collective-permute-start | bytes 245768 | tf_op jit(solution)/shard_map/cond/branch_1_fun/ppermute | solution.py:41
  39.7 0.0 collective-permute-done.21.refs_1_
  39.7 0.6 %collective-permute-start.26 = (bf16[20,16,128]{2,1,0:T(8,128)(2,1)S(1)}, bf16[20,16,128]{2,1,0:T(8,128)(2,1)S(1)}, u32[]{:S(2)}, u32[]{:S(2)}) collective-permute-start(bf16[20,16,128]{2,1,0:T(8,128)(2,1)S(1)} %get-tuple-element.137), channel_id=1, source_target_pairs={{0,20},{4,16},{8,28},{12,24},{16,4},{20,0},{24,12},{28,8},{1,21},{... | collective-permute-start | bytes 245768 | tf_op jit(solution)/shard_map/cond/branch_1_fun/ppermute | solution.py:41
  40.3 1.7 %collective-permute-done.22.refs_2_ = bf16[20,16,128]{2,1,0:T(8,128)(2,1)S(1)} collective-permute-done((bf16[20,16,128]{2,1,0:T(8,128)(2,1)S(1)}, bf16[20,16,128]{2,1,0:T(8,128)(2,1)S(1)}, u32[]{:S(2)}, u32[]{:S(2)}) %collective-permute-start.22) | collective-permute-done | bytes 81952 | tf_op jit(solution)/shard_map/cond/branch_1_fun/ppermute | solution.py:41
  42.0 0.0 collective-permute-start.27
  42.0 1.6 %collective-permute-done.23.refs_3_ = bf16[20,16,128]{2,1,0:T(8,128)(2,1)S(1)} collective-permute-done((bf16[20,16,128]{2,1,0:T(8,128)(2,1)S(1)}, bf16[20,16,128]{2,1,0:T(8,128)(2,1)S(1)}, u32[]{:S(2)}, u32[]{:S(2)}) %collective-permute-start.23) | collective-permute-done | bytes 81952 | tf_op jit(solution)/shard_map/cond/branch_1_fun/ppermute | solution.py:41
  43.6 0.0 collective-permute-done.24.refs_4_
  43.6 0.5 %collective-permute-done.25.refs_5_ = bf16[20,16,128]{2,1,0:T(8,128)(2,1)S(1)} collective-permute-done((bf16[20,16,128]{2,1,0:T(8,128)(2,1)S(1)}, bf16[20,16,128]{2,1,0:T(8,128)(2,1)S(1)}, u32[]{:S(2)}, u32[]{:S(2)}) %collective-permute-start.25) | collective-permute-done | bytes 81952 | tf_op jit(solution)/shard_map/cond/branch_1_fun/ppermute | solution.py:41
  44.1 0.9 %collective-permute-done.26.refs_6_ = bf16[20,16,128]{2,1,0:T(8,128)(2,1)S(1)} collective-permute-done((bf16[20,16,128]{2,1,0:T(8,128)(2,1)S(1)}, bf16[20,16,128]{2,1,0:T(8,128)(2,1)S(1)}, u32[]{:S(2)}, u32[]{:S(2)}) %collective-permute-start.26) | collective-permute-done | bytes 81952 | tf_op jit(solution)/shard_map/cond/branch_1_fun/ppermute | solution.py:41
  45.0 0.0 collective-permute-done.27.refs_7_
  45.0 1.6 %branch_1_fun.5 = bf16[2,2,4,8,4096]{4,3,2,1,0:T(8,128)(2,1)} custom-call(s32[4]{0:T(128)S(1)} %get-tuple-element.115.count_ref, bf16[20,16,128]{2,1,0:T(8,128)(2,1)S(1)} %get-tuple-element.131.refs_0_, bf16[20,16,128]{2,1,0:T(8,128)(2,1)S(1)} %collective-permute-done.21.refs_1_, bf16[20,16,128]{2,1,0:T(8,128)(2,1)S(1)} %collective-permute-done.22.refs_2_, ...), custom_call_target="tpu_custom_call" | custom-call | tf_op jit(solution)/shard_map/cond/branch_1_fun/pallas_call | solution.py:453
Async XLA Ops:
  0.0 7.9 %copy-start = (s32[4]{0:T(128)S(1)}, s32[4]{0:T(128)}, u32[]{:S(2)}) copy-start(s32[4]{0:T(128)} %count_ref.1) | copy-start | bytes 52
  0.0 7.9 %copy-start.1 = (s32[4,8]{1,0:T(4,128)S(1)}, s32[4,8]{1,0:T(4,128)}, u32[]{:S(2)}) copy-start(s32[4,8]{1,0:T(4,128)} %kept_ref.1) | copy-start | bytes 388
  1.3 17.9 %collective-permute-start.71 = (bf16[2,2,1,256,256]{4,3,2,1,0:T(8,128)(2,1)S(1)}, bf16[2,2,1,256,256]{4,3,2,1,0:T(8,128)(2,1)S(1)}, u32[]{:S(2)}, u32[]{:S(2)}) collective-permute-start(bf16[2,2,1,256,256]{4,3,2,1,0:T(8,128)(2,1)S(1)} %get-tuple-element.222), channel_id=1, source_target_pairs={{1,2},{2,1},{5,6},{6,5},{9,10},{10,9},{13,14},{14,13},{17,18},{18,... | collective-permute-start | bytes 1572872 | tf_op jit(solution)/shard_map/ppermute | solution.py:475
  2.0 17.5 %collective-permute-start.70 = (bf16[2,2,1,256,256]{4,3,2,1,0:T(8,128)(2,1)S(1)}, bf16[2,2,1,256,256]{4,3,2,1,0:T(8,128)(2,1)S(1)}, u32[]{:S(2)}, u32[]{:S(2)}) collective-permute-start(bf16[2,2,1,256,256]{4,3,2,1,0:T(8,128)(2,1)S(1)} %get-tuple-element.223), channel_id=1, source_target_pairs={{0,1},{2,3},{1,0},{3,2},{4,5},{6,7},{5,4},{7,6},{8,9},{10,11},{9,8... | collective-permute-start | bytes 1572872 | tf_op jit(solution)/shard_map/ppermute | solution.py:475
  22.3 5.7 %collective-permute-start.14 = (bf16[20,16,128]{2,1,0:T(8,128)(2,1)S(1)}, bf16[20,16,128]{2,1,0:T(8,128)(2,1)S(1)}, u32[]{:S(2)}, u32[]{:S(2)}) collective-permute-start(bf16[20,16,128]{2,1,0:T(8,128)(2,1)S(1)} %get-tuple-element.124), channel_id=1, source_target_pairs={{0,24},{4,28},{8,16},{12,20},{16,8},{20,12},{24,0},{28,4},{1,25},{... | collective-permute-start | bytes 245768 | tf_op jit(solution)/shard_map/cond/branch_1_fun/ppermute | solution.py:41
  24.8 5.6 %collective-permute-start.15 = (bf16[20,16,128]{2,1,0:T(8,128)(2,1)S(1)}, bf16[20,16,128]{2,1,0:T(8,128)(2,1)S(1)}, u32[]{:S(2)}, u32[]{:S(2)}) collective-permute-start(bf16[20,16,128]{2,1,0:T(8,128)(2,1)S(1)} %get-tuple-element.125), channel_id=1, source_target_pairs={{0,28},{4,24},{8,20},{12,16},{16,12},{20,8},{24,4},{28,0},{1,29},{... | collective-permute-start | bytes 245768 | tf_op jit(solution)/shard_map/cond/branch_1_fun/ppermute | solution.py:41
  24.8 6.5 %collective-permute-start.16 = (bf16[20,16,128]{2,1,0:T(8,128)(2,1)S(1)}, bf16[20,16,128]{2,1,0:T(8,128)(2,1)S(1)}, u32[]{:S(2)}, u32[]{:S(2)}) collective-permute-start(bf16[20,16,128]{2,1,0:T(8,128)(2,1)S(1)} %get-tuple-element.126), channel_id=1, source_target_pairs={{0,8},{4,12},{8,0},{12,4},{16,24},{20,28},{24,16},{28,20},{1,9},{5... | collective-permute-start | bytes 245768 | tf_op jit(solution)/shard_map/cond/branch_1_fun/ppermute | solution.py:41
  25.4 6.0 %collective-permute-start.17 = (bf16[20,16,128]{2,1,0:T(8,128)(2,1)S(1)}, bf16[20,16,128]{2,1,0:T(8,128)(2,1)S(1)}, u32[]{:S(2)}, u32[]{:S(2)}) collective-permute-start(bf16[20,16,128]{2,1,0:T(8,128)(2,1)S(1)} %get-tuple-element.127), channel_id=1, source_target_pairs={{0,16},{4,20},{8,24},{12,28},{16,0},{20,4},{24,8},{28,12},{1,17},{... | collective-permute-start | bytes 245768 | tf_op jit(solution)/shard_map/cond/branch_1_fun/ppermute | solution.py:41
  26.7 6.3 %collective-permute-start.18 = (bf16[20,16,128]{2,1,0:T(8,128)(2,1)S(1)}, bf16[20,16,128]{2,1,0:T(8,128)(2,1)S(1)}, u32[]{:S(2)}, u32[]{:S(2)}) collective-permute-start(bf16[20,16,128]{2,1,0:T(8,128)(2,1)S(1)} %get-tuple-element.128), channel_id=1, source_target_pairs={{0,12},{4,8},{8,4},{12,0},{16,28},{20,24},{24,20},{28,16},{1,13},{... | collective-permute-start | bytes 245768 | tf_op jit(solution)/shard_map/cond/branch_1_fun/ppermute | solution.py:41
  28.0 5.2 %collective-permute-start.19 = (bf16[20,16,128]{2,1,0:T(8,128)(2,1)S(1)}, bf16[20,16,128]{2,1,0:T(8,128)(2,1)S(1)}, u32[]{:S(2)}, u32[]{:S(2)}) collective-permute-start(bf16[20,16,128]{2,1,0:T(8,128)(2,1)S(1)} %get-tuple-element.129), channel_id=1, source_target_pairs={{0,20},{4,16},{8,28},{12,24},{16,4},{20,0},{24,12},{28,8},{1,21},{... | collective-permute-start | bytes 245768 | tf_op jit(solution)/shard_map/cond/branch_1_fun/ppermute | solution.py:41
  30.5 2.8 %collective-permute-start.20 = (bf16[20,16,128]{2,1,0:T(8,128)(2,1)S(1)}, bf16[20,16,128]{2,1,0:T(8,128)(2,1)S(1)}, u32[]{:S(2)}, u32[]{:S(2)}) collective-permute-start(bf16[20,16,128]{2,1,0:T(8,128)(2,1)S(1)} %get-tuple-element.130), channel_id=1, source_target_pairs={{0,4},{4,0},{8,12},{12,8},{16,20},{20,16},{24,28},{28,24},{1,5},{5... | collective-permute-start | bytes 245768 | tf_op jit(solution)/shard_map/cond/branch_1_fun/ppermute | solution.py:41
  34.2 5.5 %collective-permute-start.21 = (bf16[20,16,128]{2,1,0:T(8,128)(2,1)S(1)}, bf16[20,16,128]{2,1,0:T(8,128)(2,1)S(1)}, u32[]{:S(2)}, u32[]{:S(2)}) collective-permute-start(bf16[20,16,128]{2,1,0:T(8,128)(2,1)S(1)} %get-tuple-element.132), channel_id=1, source_target_pairs={{0,24},{4,28},{8,16},{12,20},{16,8},{20,12},{24,0},{28,4},{1,25},{... | collective-permute-start | bytes 245768 | tf_op jit(solution)/shard_map/cond/branch_1_fun/ppermute | solution.py:41
  36.4 5.6 %collective-permute-start.22 = (bf16[20,16,128]{2,1,0:T(8,128)(2,1)S(1)}, bf16[20,16,128]{2,1,0:T(8,128)(2,1)S(1)}, u32[]{:S(2)}, u32[]{:S(2)}) collective-permute-start(bf16[20,16,128]{2,1,0:T(8,128)(2,1)S(1)} %get-tuple-element.133), channel_id=1, source_target_pairs={{0,28},{4,24},{8,20},{12,16},{16,12},{20,8},{24,4},{28,0},{1,29},{... | collective-permute-start | bytes 245768 | tf_op jit(solution)/shard_map/cond/branch_1_fun/ppermute | solution.py:41
  36.5 7.0 %collective-permute-start.23 = (bf16[20,16,128]{2,1,0:T(8,128)(2,1)S(1)}, bf16[20,16,128]{2,1,0:T(8,128)(2,1)S(1)}, u32[]{:S(2)}, u32[]{:S(2)}) collective-permute-start(bf16[20,16,128]{2,1,0:T(8,128)(2,1)S(1)} %get-tuple-element.134), channel_id=1, source_target_pairs={{0,8},{4,12},{8,0},{12,4},{16,24},{20,28},{24,16},{28,20},{1,9},{5... | collective-permute-start | bytes 245768 | tf_op jit(solution)/shard_map/cond/branch_1_fun/ppermute | solution.py:41
  37.6 6.0 %collective-permute-start.24 = (bf16[20,16,128]{2,1,0:T(8,128)(2,1)S(1)}, bf16[20,16,128]{2,1,0:T(8,128)(2,1)S(1)}, u32[]{:S(2)}, u32[]{:S(2)}) collective-permute-start(bf16[20,16,128]{2,1,0:T(8,128)(2,1)S(1)} %get-tuple-element.135), channel_id=1, source_target_pairs={{0,16},{4,20},{8,24},{12,28},{16,0},{20,4},{24,8},{28,12},{1,17},{... | collective-permute-start | bytes 245768 | tf_op jit(solution)/shard_map/cond/branch_1_fun/ppermute | solution.py:41
  38.8 5.3 %collective-permute-start.25 = (bf16[20,16,128]{2,1,0:T(8,128)(2,1)S(1)}, bf16[20,16,128]{2,1,0:T(8,128)(2,1)S(1)}, u32[]{:S(2)}, u32[]{:S(2)}) collective-permute-start(bf16[20,16,128]{2,1,0:T(8,128)(2,1)S(1)} %get-tuple-element.136), channel_id=1, source_target_pairs={{0,12},{4,8},{8,4},{12,0},{16,28},{20,24},{24,20},{28,16},{1,13},{... | collective-permute-start | bytes 245768 | tf_op jit(solution)/shard_map/cond/branch_1_fun/ppermute | solution.py:41
  39.7 5.3 %collective-permute-start.26 = (bf16[20,16,128]{2,1,0:T(8,128)(2,1)S(1)}, bf16[20,16,128]{2,1,0:T(8,128)(2,1)S(1)}, u32[]{:S(2)}, u32[]{:S(2)}) collective-permute-start(bf16[20,16,128]{2,1,0:T(8,128)(2,1)S(1)} %get-tuple-element.137), channel_id=1, source_target_pairs={{0,20},{4,16},{8,28},{12,24},{16,4},{20,0},{24,12},{28,8},{1,21},{... | collective-permute-start | bytes 245768 | tf_op jit(solution)/shard_map/cond/branch_1_fun/ppermute | solution.py:41
  42.0 3.0 %collective-permute-start.27 = (bf16[20,16,128]{2,1,0:T(8,128)(2,1)S(1)}, bf16[20,16,128]{2,1,0:T(8,128)(2,1)S(1)}, u32[]{:S(2)}, u32[]{:S(2)}) collective-permute-start(bf16[20,16,128]{2,1,0:T(8,128)(2,1)S(1)} %get-tuple-element.138), channel_id=1, source_target_pairs={{0,4},{4,0},{8,12},{12,8},{16,20},{20,16},{24,28},{28,24},{1,5},{5... | collective-permute-start | bytes 245768 | tf_op jit(solution)/shard_map/cond/branch_1_fun/ppermute | solution.py:41
